TPU v7x, 512 devices: a whole 4x8x8 slice. The times are simulated.
512 devices in a mesh: gx: 16 (over x, y_hi), gy: 32 (over z, y_lo, core).
Axes of the slice: x: 4, y: 8 (y_hi: 4, y_lo: 2; y = y_hi * 2 + y_lo), z: 8, core: 2. Of those that a mesh axis runs over, the one named last changes fastest.
Arguments:
- spectra: bfloat16 [114688, 1024], P(('gx', 'gy')), may hold values from -16 to 16
- scores: bfloat16 [114688, 32], P(('gx', 'gy')), may hold values from -0.5 to 1.5
Outputs:
- product: float32 [114688, 32], P(('gx', 'gy'))
All inputs are finite; a program needn't handle non-finite values.
Results may differ from a plain program's by a relative error of at most 0.0003.
Values may be sent and summed in bfloat16 or wider, within the bound.
No kernel may reach another device: no remote copies, remote signals or barrier semaphores. Data moves between devices by JAX's collectives and lax.ppermute only.
A program may use at most 64 MiB of HBM per device.

v0:
```python
import functools

import jax
import jax.numpy as jnp
from jax import lax
from jax.experimental import pallas as pl
from jax.experimental.pallas import tpu as pltpu
from jax.sharding import PartitionSpec as P

WAVE = 1024
BLK = 224
COLS = 32
PACK = 16
AXES = ("gx", "gy")

spread_rate = 4.0


def split(i):
    return i >> 2, (i >> 1) & 1, i & 1


def device(quad, side, core, quads):
    return (quad % quads) * 4 + side * 2 + core


def stepped(i, j, quads):
    quad, side, core = split(i)
    return device(quad + j, side, core, quads)


def within(i, j, column, quads):
    return stepped(i, j, quads) // (4 * column) == i // (4 * column)


def near_source(i, j, steps, column, quads):
    return stepped(i, j, quads) if within(i, j * steps, column, quads) else None


def inner_source(i, j, column, quads):
    return stepped(i, j, quads) if within(i, j, column, quads) else None


def far_source(i, column, quads):
    for j in (2, -2):
        if not within(i, j, column, quads):
            return stepped(i, j, quads)
    return None


def back_level(me, column):
    level = (me >> 2) % column
    return (level == 1) | (level == column - 2)


def back_source(i, column, quads):
    for j in (1, -1):
        if not within(i, j, column, quads):
            return stepped(i, -j, quads)
    return None


def sources(source_of, n, column):
    found = [(source_of(i, column, n // 4), i) for i in range(n)]
    return [(source, i) for source, i in found if source is not None]


VMEM = pl.BlockSpec(memory_space=pltpu.VMEM)
ROW = jax.ShapeDtypeStruct((1, BLK), jnp.float32)


def packed_body(spectra_ref, scores_ref, out_ref):
    out_ref[0:BLK, :] = spectra_ref[...]
    turned = scores_ref[...].astype(jnp.float32).T.astype(jnp.bfloat16)
    out_ref[BLK:BLK + PACK, :] = jnp.zeros((PACK, WAVE), jnp.bfloat16)
    out_ref[BLK:BLK + PACK, 0:BLK] = turned[0:PACK]
    out_ref[BLK:BLK + PACK, 256:256 + BLK] = turned[PACK:COLS]


def packed(spectra, scores):
    return pl.pallas_call(
        packed_body,
        out_shape=jax.ShapeDtypeStruct((BLK + PACK, WAVE), jnp.bfloat16),
        in_specs=[VMEM] * 2,
        out_specs=VMEM,
        compiler_params=pltpu.CompilerParams(vmem_limit_bytes=12 * 1024 * 1024),
        cost_estimate=pl.CostEstimate(flops=0, bytes_accessed=4 * BLK * WAVE, transcendentals=0),
    )(spectra, scores)


def pick_body(which_ref, one_ref, other_ref, out_ref):
    @pl.when(which_ref[0] != 0)
    def _():
        out_ref[...] = one_ref[...]

    @pl.when(which_ref[0] == 0)
    def _():
        out_ref[...] = other_ref[...]


def pick(which, one, other):
    return pl.pallas_call(
        pick_body,
        out_shape=jax.ShapeDtypeStruct(one.shape, one.dtype),
        in_specs=[pl.BlockSpec(memory_space=pltpu.SMEM)] + [VMEM] * 2,
        out_specs=VMEM,
        compiler_params=pltpu.CompilerParams(vmem_limit_bytes=12 * 1024 * 1024),
        cost_estimate=pl.CostEstimate(flops=0, bytes_accessed=4 * BLK * WAVE, transcendentals=0),
    )(which.astype(jnp.int32).reshape(1), one, other)


def rows_of(ref):
    return ref[0:BLK, :]


def scores_of(ref):
    return jnp.concatenate([ref[BLK:BLK + PACK, 0:BLK], ref[BLK:BLK + PACK, 256:256 + BLK]], axis=0)


def norms_of(ref):
    x = rows_of(ref).astype(jnp.float32)
    column = jnp.sum(x * x, axis=1, keepdims=True)
    row = jnp.broadcast_to(column, (BLK, 128)).T[0:1, :]
    return column, row


def tile_of(a_ref, a_column, b_ref, b_row):
    cross = lax.dot_general(
        rows_of(a_ref), rows_of(b_ref), (((1,), (1,)), ((), ())), preferred_element_type=jnp.float32
    )
    dist = a_column + b_row - 2.0 * cross
    return jnp.exp(-spread_rate * dist / WAVE).astype(jnp.bfloat16)


def to_rows(kern, b_scores):
    return lax.dot_general(b_scores, kern, (((1,), (1,)), ((), ())), preferred_element_type=jnp.float32)


def to_columns(kern, a_scores):
    return jnp.dot(a_scores, kern, preferred_element_type=jnp.float32)


def pairs_body(tiles, outs, known, rows, *refs):
    count = len(refs) - len(outs) - len(known) - len(rows)
    blocks, before, totals = refs[:count], refs[count:count + len(known)], refs[count + len(known):]
    used = sorted({t for tile in tiles for t in tile})
    norms = {t: norms_of(blocks[t]) for t in used}
    scores = {t: scores_of(blocks[t]) for t in used}
    sums = {t: ref[...] for t, ref in zip(known, before)}

    def add(t, value):
        sums[t] = value if t not in sums else sums[t] + value

    for a, b in tiles:
        kern = tile_of(blocks[a], norms[a][0], blocks[b], norms[b][1])
        add(a, to_rows(kern, scores[b]))
        if a != b:
            add(b, to_columns(kern, scores[a]))
    for t, total in zip(outs, totals):
        total[...] = sums[t]
    for t, row in zip(rows, totals[len(outs):]):
        row[...] = norms[t][1]


def cost(tiles, blocks):
    return pl.CostEstimate(
        flops=tiles * 2 * BLK * BLK * (WAVE + 2 * COLS),
        bytes_accessed=blocks * (BLK + PACK) * WAVE * 2,
        transcendentals=tiles * BLK * BLK,
    )


def pairs(blocks, tiles, outs, known, rows, sums):
    return pl.pallas_call(
        functools.partial(pairs_body, tiles, outs, known, rows),
        out_shape=[jax.ShapeDtypeStruct((COLS, BLK), jnp.float32)] * len(outs) + [ROW] * len(rows),
        in_specs=[VMEM] * (len(blocks) + len(sums)),
        out_specs=[VMEM] * (len(outs) + len(rows)),
        compiler_params=pltpu.CompilerParams(vmem_limit_bytes=12 * 1024 * 1024),
        cost_estimate=cost(len(tiles), len(blocks)),
    )(*blocks, *sums)


def extra_body(
    low_ref, extra_ref, zero_ref, up_ref, down_ref, up2_ref, down2_ref,
    zero_norms, up_norms, down_norms, up2_norms, down2_norms,
    zero_in, up_in, down_in, up2_in, down2_in,
    zero_total, up_total, down_total, up2_total, down2_total, extra_total,
):
    column, _ = norms_of(extra_ref)
    extra_scores = scores_of(extra_ref)

    def one(ref, norms, before, after):
        kern = tile_of(extra_ref, column, ref, norms[...])
        after[...] = before[...] + to_columns(kern, extra_scores)
        return to_rows(kern, scores_of(ref))

    mine = one(zero_ref, zero_norms, zero_in, zero_total)
    mine = mine + one(up_ref, up_norms, up_in, up_total)
    extra_total[...] = mine + one(down_ref, down_norms, down_in, down_total)

    @pl.when(low_ref[0] != 0)
    def _():
        extra_total[...] += one(up2_ref, up2_norms, up2_in, up2_total)
        down2_total[...] = down2_in[...]

    @pl.when(low_ref[0] == 0)
    def _():
        extra_total[...] += one(down2_ref, down2_norms, down2_in, down2_total)
        up2_total[...] = up2_in[...]


def extra_pairs(is_low, extra, blocks, norms, sums):
    total = jax.ShapeDtypeStruct((COLS, BLK), jnp.float32)
    outs = pl.pallas_call(
        extra_body,
        out_shape=[total] * 6,
        in_specs=[pl.BlockSpec(memory_space=pltpu.SMEM)] + [VMEM] * 16,
        out_specs=[VMEM] * 6,
        compiler_params=pltpu.CompilerParams(vmem_limit_bytes=12 * 1024 * 1024),
        cost_estimate=cost(4, 6),
    )(is_low.astype(jnp.int32).reshape(1), extra, *blocks, *norms, *sums)
    return outs[:5], outs[5]


def early_body(low_ref, extra_ref, zero_ref, up2_ref, down2_ref,
               zero_total, up2_total, down2_total, extra_total, zero_norms, up2_norms, down2_norms, chosen_ref):
    low = low_ref[0] != 0

    @pl.when(low)
    def _():
        chosen_ref[...] = up2_ref[...]

    @pl.when(jnp.logical_not(low))
    def _():
        chosen_ref[...] = down2_ref[...]

    zero_column, zero_row = norms_of(zero_ref)
    zero_scores = scores_of(zero_ref)
    total = to_rows(tile_of(zero_ref, zero_column, zero_ref, zero_row), zero_scores)
    _, up2_row = norms_of(up2_ref)
    down2_column, down2_row = norms_of(down2_ref)
    zero_norms[...], up2_norms[...], down2_norms[...] = zero_row, up2_row, down2_row
    kern = tile_of(down2_ref, down2_column, up2_ref, up2_row)
    down2_sum = to_rows(kern, scores_of(up2_ref))
    up2_sum = to_columns(kern, scores_of(down2_ref))
    column, _ = norms_of(extra_ref)
    scores = scores_of(extra_ref)
    kern = tile_of(extra_ref, column, zero_ref, zero_row)
    mine = to_rows(kern, zero_scores)
    zero_total[...] = total + to_columns(kern, scores)
    kern = tile_of(extra_ref, column, chosen_ref, jnp.where(low, up2_row, down2_row))
    extra_total[...] = mine + to_rows(kern, scores_of(chosen_ref))
    theirs = to_columns(kern, scores)
    up2_total[...] = up2_sum + jnp.where(low, theirs, 0.0)
    down2_total[...] = down2_sum + jnp.where(low, 0.0, theirs)


def early_pairs(is_low, blocks):
    return pl.pallas_call(
        early_body,
        out_shape=[jax.ShapeDtypeStruct((COLS, BLK), jnp.float32)] * 4 + [ROW] * 3,
        in_specs=[pl.BlockSpec(memory_space=pltpu.SMEM)] + [VMEM] * 4,
        out_specs=[VMEM] * 7,
        scratch_shapes=[pltpu.VMEM((BLK + PACK, WAVE), jnp.bfloat16)],
        compiler_params=pltpu.CompilerParams(vmem_limit_bytes=12 * 1024 * 1024),
        cost_estimate=cost(4, 4),
    )(is_low.astype(jnp.int32).reshape(1), *blocks)


def on_device(spectra, scores):
    n = lax.axis_size(AXES)
    quads = n // 4
    me = lax.axis_index(AXES)
    column = lax.axis_size("gy") // 4
    level = (me >> 2) % column
    low, high = level < 2, level >= column - 2
    def route(block, source_of):
        return lax.ppermute(block, AXES, sources(source_of, n, column))

    def send(block, source_of):
        return lax.ppermute(block, AXES, [(i, source) for source, i in sources(source_of, n, column)])

    def swap(block, bits):
        return lax.ppermute(block, AXES, [(i, i ^ bits) for i in range(n)])

    zero = packed(spectra, scores)
    far = route(zero, far_source)
    up = route(zero, lambda i, column, quads: near_source(i, 1, 1, column, quads))
    down = route(zero, lambda i, column, quads: near_source(i, -1, 1, column, quads))
    up2 = route(up, lambda i, column, quads: near_source(i, 1, 2, column, quads))
    down2 = route(down, lambda i, column, quads: near_source(i, -1, 2, column, quads))
    back = route(jnp.where(back_level(me, column), far, up2), back_source)
    up2 = pick(high, far, up2)
    beside = swap(up2, 2)
    sibling = swap(up2, 1)
    across = swap(beside, 1)
    up2, down2 = lax.optimization_barrier((up2, down2))
    down2 = jnp.where(low, far, down2)
    back, _, _ = lax.optimization_barrier((back, up2, down2))
    up = pick(level == column - 1, back, up)
    down = pick(level == 0, back, down)

    total, two, eight, for_sibling, zero_norms, up2_norms, down2_norms = early_pairs(
        (me & 1) == 0, [sibling, zero, up2, down2]
    )
    total, one, nine, two, for_sibling, up_norms, down_norms = pairs(
        [zero, up, down, up2, sibling],
        ((0, 1), (2, 1), (2, 3), (4, 1), (4, 2)),
        (0, 1, 2, 3, 4),
        (0, 3, 4),
        (1, 2),
        [total, two, for_sibling],
    )
    blocks = [zero, up, down, up2, down2]
    norms = [zero_norms, up_norms, down_norms, up2_norms, down2_norms]
    sums, for_beside = extra_pairs((me & 2) == 0, beside, blocks, norms, [total, one, nine, two, eight])
    sums, for_across = extra_pairs((me & 2) == 0, across, blocks, norms, sums)
    total, one, nine, two, eight = sums
    handed = swap(jnp.concatenate([for_sibling, for_across]), 1)
    two = two + handed[:COLS] + swap(for_beside + handed[COLS:], 2)

    none = jnp.zeros_like(one)
    upward = send(
        jnp.concatenate([one, jnp.where(level == 0, nine, none)]),
        lambda i, column, quads: near_source(i, 1, 1, column, quads),
    )
    downward = send(
        jnp.concatenate([nine, jnp.where(level == column - 1, one, none)]),
        lambda i, column, quads: near_source(i, -1, 1, column, quads),
    )
    total = total + upward[:COLS] + downward[:COLS]
    crossing = jnp.where(high, two + downward[COLS:], eight + upward[COLS:])
    far_sums = send(eight, lambda i, column, quads: inner_source(i, -2, column, quads))
    far_sums = far_sums + send(two, lambda i, column, quads: inner_source(i, 2, column, quads))
    total = total + send(crossing, far_source) + far_sums
    return total.T


def solution(mesh):
    return jax.shard_map(
        on_device,
        mesh=mesh,
        in_specs=(P(AXES, None), P(AXES, None)),
        out_specs=P(AXES, None),
        check_vma=False,
    )
```

profile of v0, /device:TPU:8, one launch (start us, length us, event | category | flops | bytes accessed | tf_op | source)
XLA Modules:
  0.0 100.2 jit_solution(5371048714984983702)
XLA Ops:
  1.9 1.3 %collective-permute-start.1 = (bf16[240,1024]{1,0:T(8,128)(2,1)S(1)}, bf16[240,1024]{1,0:T(8,128)(2,1)S(1)}, u32[]{:S(2)}, u32[]{:S(2)}) collective-permute-start(bf16[240,1024]{1,0:T(8,128)(2,1)S(1)} %shard_map.28.zero_ref.refs_0_), channel_id=1, source_target_pairs={{4,0},{5,1},{6,2},{7,3},{8,4},{9,5},{10,6},{11,7},{12,8},{13,9},{1... | collective-permute-start | bytes 1474568 | tf_op jit(solution)/shard_map/ppermute | solution.py:279
  3.2 4.9 %collective-permute-start.6 = (bf16[240,1024]{1,0:T(8,128)(2,1)S(1)}, bf16[240,1024]{1,0:T(8,128)(2,1)S(1)}, u32[]{:S(2)}, u32[]{:S(2)}) collective-permute-start(bf16[240,1024]{1,0:T(8,128)(2,1)S(1)} %shard_map.28.zero_ref.refs_0_), channel_id=1, source_target_pairs={{0,4},{1,5},{2,6},{3,7},{4,8},{5,9},{6,10},{7,11},{8,12},{9,13},{1... | collective-permute-start | bytes 1474568 | tf_op jit(solution)/shard_map/ppermute | solution.py:279
  8.2 15.6 %collective-permute-start = (bf16[240,1024]{1,0:T(8,128)(2,1)S(1)}, bf16[240,1024]{1,0:T(8,128)(2,1)S(1)}, u32[]{:S(2)}, u32[]{:S(2)}) collective-permute-start(bf16[240,1024]{1,0:T(8,128)(2,1)S(1)} %shard_map.28.zero_ref.refs_0_), channel_id=1, source_target_pairs={{504,0},{505,1},{506,2},{507,3},{508,4},{509,5},{510,6},{511,7},{3... | collective-permute-start | bytes 1474568 | tf_op jit(solution)/shard_map/ppermute | solution.py:279
  23.8 1.3 %collective-permute-start.2 = (bf16[240,1024]{1,0:T(8,128)(2,1)S(1)}, bf16[240,1024]{1,0:T(8,128)(2,1)S(1)}, u32[]{:S(2)}, u32[]{:S(2)}) collective-permute-start(bf16[240,1024]{1,0:T(8,128)(2,1)S(1)} %collective-permute-done.1.other_ref), channel_id=1, source_target_pairs={{4,0},{5,1},{6,2},{7,3},{8,4},{9,5},{10,6},{11,7},{12,8},{13,9},{1... | collective-permute-start | bytes 1474568 | tf_op jit(solution)/shard_map/ppermute | solution.py:279
  26.6 18.4 %collective-permute-done.one_ref = bf16[240,1024]{1,0:T(8,128)(2,1)S(1)} collective-permute-done((bf16[240,1024]{1,0:T(8,128)(2,1)S(1)}, bf16[240,1024]{1,0:T(8,128)(2,1)S(1)}, u32[]{:S(2)}, u32[]{:S(2)}) %collective-permute-start) | collective-permute-done | bytes 491552 | tf_op jit(solution)/shard_map/ppermute | solution.py:279
  45.0 3.4 %collective-permute-start.3 = (bf16[240,1024]{1,0:T(8,128)(2,1)S(1)}, bf16[240,1024]{1,0:T(8,128)(2,1)S(1)}, u32[]{:S(2)}, u32[]{:S(2)}) collective-permute-start(bf16[240,1024]{1,0:T(8,128)(2,1)S(1)} %shard_map.29.up2_ref.refs_3_), channel_id=1, source_target_pairs={{0,2},{1,3},{2,0},{3,1},{4,6},{5,7},{6,4},{7,5},{8,10},{9,11},{10,... | collective-permute-start | bytes 1474568 | tf_op jit(solution)/shard_map/ppermute | solution.py:285
  49.3 1.3 %collective-permute-start.5 = (bf16[240,1024]{1,0:T(8,128)(2,1)}, bf16[240,1024]{1,0:T(8,128)(2,1)S(1)}, u32[]{:S(2)}, u32[]{:S(2)}) collective-permute-start(bf16[240,1024]{1,0:T(8,128)(2,1)} %get-tuple-element.66), channel_id=1, source_target_pairs={{4,0},{5,1},{6,2},{7,3},{24,28},{25,29},{26,30},{27,31},{36,32},{3... | collective-permute-start | bytes 1474568 | tf_op jit(solution)/shard_map/ppermute | solution.py:279
  50.6 1.9 %collective-permute-start.8 = (bf16[240,1024]{1,0:T(8,128)(2,1)S(1)}, bf16[240,1024]{1,0:T(8,128)(2,1)S(1)}, u32[]{:S(2)}, u32[]{:S(2)}) collective-permute-start(bf16[240,1024]{1,0:T(8,128)(2,1)S(1)} %shard_map.29.up2_ref.refs_3_), channel_id=1, source_target_pairs={{0,1},{1,0},{2,3},{3,2},{4,5},{5,4},{6,7},{7,6},{8,9},{9,8},{10,11... | collective-permute-start | bytes 1474568 | tf_op jit(solution)/shard_map/ppermute | solution.py:285
  52.5 6.6 %collective-permute-done.3.extra_ref = bf16[240,1024]{1,0:T(8,128)(2,1)S(1)} collective-permute-done((bf16[240,1024]{1,0:T(8,128)(2,1)S(1)}, bf16[240,1024]{1,0:T(8,128)(2,1)S(1)}, u32[]{:S(2)}, u32[]{:S(2)}) %collective-permute-start.3) | collective-permute-done | bytes 491552 | tf_op jit(solution)/shard_map/ppermute | solution.py:285
  59.2 1.9 %collective-permute-start.4 = (bf16[240,1024]{1,0:T(8,128)(2,1)S(1)}, bf16[240,1024]{1,0:T(8,128)(2,1)S(1)}, u32[]{:S(2)}, u32[]{:S(2)}) collective-permute-start(bf16[240,1024]{1,0:T(8,128)(2,1)S(1)} %collective-permute-done.3.extra_ref), channel_id=1, source_target_pairs={{0,1},{1,0},{2,3},{3,2},{4,5},{5,4},{6,7},{7,6},{8,9},{9,8},{10,11... | collective-permute-start | bytes 1474568 | tf_op jit(solution)/shard_map/ppermute | solution.py:285
  61.1 2.2 %collective-permute-done.5.one_ref = bf16[240,1024]{1,0:T(8,128)(2,1)S(1)} collective-permute-done((bf16[240,1024]{1,0:T(8,128)(2,1)}, bf16[240,1024]{1,0:T(8,128)(2,1)S(1)}, u32[]{:S(2)}, u32[]{:S(2)}) %collective-permute-start.5) | collective-permute-done | bytes 491552 | tf_op jit(solution)/shard_map/ppermute | solution.py:279
  65.4 1.6 %shard_map.32 = (f32[32,224]{1,0:T(8,128)S(1)}, f32[32,224]{1,0:T(8,128)S(1)}, f32[32,224]{1,0:T(8,128)S(1)}, f32[32,224]{1,0:T(8,128)S(1)}, f32[1,224]{1,0:T(1,...) custom-call(s32[1]{0:T(128)} %bitcast.4.low_ref, bf16[240,1024]{1,0:T(8,128)(2,1)S(1)} %collective-permute-done.8.extra_ref.refs_4_, ...), custom_call_target="tpu_custom_call" | custom-call | flops 436731904 | bytes 1966080 | tf_op jit(solution)/shard_map/pallas_call | solution.py:260
  67.0 2.0 %shard_map.33 = (f32[32,224]{1,0:T(8,128)S(1)}, f32[32,224]{1,0:T(8,128)S(1)}, f32[32,224]{1,0:T(8,128)S(1)}, f32[32,224]{1,0:T(8,128)S(1)}, f32[32,224]{1,0:T(8...) custom-call(bf16[240,1024]{1,0:T(8,128)(2,1)S(1)} %shard_map.28.zero_ref.refs_0_, ...), custom_call_target="tpu_custom_call" | custom-call | flops 545914880 | bytes 2457600 | tf_op jit(solution)/shard_map/pallas_call | solution.py:174
  69.0 1.7 %shard_map.34 = (f32[32,224]{1,0:T(8,128)S(1)}, f32[32,224]{1,0:T(8,128)S(1)}, f32[32,224]{1,0:T(8,128)S(1)}, f32[32,224]{1,0:T(8,128)S(1)}, f32[32,224]{1,0:T(8,128)S(1)}, /*index=5*/f32[32,224]{1,0:T(8,128)S(1)}) custom-call(s32[1]{0:T(128)} %bitcast.low_ref, bf16[240,1024]{1,0:T(8,128)(2,1)S(1)} %collective-permute-done.3.extra_ref, ...), custom_call_target="tpu_custom_call" | custom-call | flops 436731904 | bytes 2949120 | tf_op jit(solution)/shard_map/pallas_call | solution.py:215
  70.7 1.7 %shard_map.35 = (f32[32,224]{1,0:T(8,128)S(1)}, f32[32,224]{1,0:T(8,128)S(1)}, f32[32,224]{1,0:T(8,128)S(1)}, f32[32,224]{1,0:T(8,128)S(1)}, f32[32,224]{1,0:T(8,128)S(1)}, /*index=5*/f32[32,224]{1,0:T(8,128)S(1)}) custom-call(s32[1]{0:T(128)} %bitcast.low_ref, bf16[240,1024]{1,0:T(8,128)(2,1)S(1)} %collective-permute-done.4.extra_ref, ...), custom_call_target="tpu_custom_call" | custom-call | flops 436731904 | bytes 2949120 | tf_op jit(solution)/shard_map/pallas_call | solution.py:215
  72.5 1.9 %collective-permute-start.11 = (f32[64,224]{1,0:T(8,128)S(1)}, f32[64,224]{1,0:T(8,128)S(1)}, u32[]{:S(2)}, u32[]{:S(2)}) collective-permute-start(f32[64,224]{1,0:T(8,128)S(1)} %pad_maximum_fusion.2), channel_id=1, source_target_pairs={{0,1},{1,0},{2,3},{3,2},{4,5},{5,4},{6,7},{7,6},{8,9},{9,8},{10,11... | collective-permute-start | bytes 172040 | tf_op jit(solution)/shard_map/ppermute | solution.py:285
  74.5 1.3 %collective-permute-start.10 = (f32[64,224]{1,0:T(8,128)S(1)}, f32[64,224]{1,0:T(8,128)S(1)}, u32[]{:S(2)}, u32[]{:S(2)}) collective-permute-start(f32[64,224]{1,0:T(8,128)S(1)} %pad_maximum_fusion.1), channel_id=1, source_target_pairs={{4,0},{5,1},{6,2},{7,3},{8,4},{9,5},{10,6},{11,7},{12,8},{13,9},{1... | collective-permute-start | bytes 172040 | tf_op jit(solution)/shard_map/ppermute | solution.py:282
  75.8 4.5 %collective-permute-start.9 = (f32[64,224]{1,0:T(8,128)S(1)}, f32[64,224]{1,0:T(8,128)S(1)}, u32[]{:S(2)}, u32[]{:S(2)}) collective-permute-start(f32[64,224]{1,0:T(8,128)S(1)} %pad_maximum_fusion), channel_id=1, source_target_pairs={{0,4},{1,5},{2,6},{3,7},{4,8},{5,9},{6,10},{7,11},{8,12},{9,13},{1... | collective-permute-start | bytes 172040 | tf_op jit(solution)/shard_map/ppermute | solution.py:282
  80.4 2.5 %collective-permute-start.12 = (f32[32,224]{1,0:T(8,128)S(1)}, f32[32,224]{1,0:T(8,128)S(1)}, u32[]{:S(2)}, u32[]{:S(2)}) collective-permute-start(f32[32,224]{1,0:T(8,128)S(1)} %slice_add_fusion.2), channel_id=1, source_target_pairs={{0,2},{1,3},{2,0},{3,1},{4,6},{5,7},{6,4},{7,5},{8,10},{9,11},{10,... | collective-permute-start | bytes 86024 | tf_op jit(solution)/shard_map/ppermute | solution.py:285
  82.9 1.3 %collective-permute-start.14 = (f32[32,224]{1,0:T(8,128)S(1)}, f32[32,224]{1,0:T(8,128)S(1)}, u32[]{:S(2)}, u32[]{:S(2)}) collective-permute-start(f32[32,224]{1,0:T(8,128)S(1)} %get-tuple-element.62), channel_id=1, source_target_pairs={{8,0},{9,1},{10,2},{11,3},{12,4},{13,5},{14,6},{15,7},{16,8},{17,9... | collective-permute-start | bytes 86024 | tf_op jit(solution)/shard_map/ppermute | solution.py:282
  84.2 1.9 %collective-permute-done.12 = f32[32,224]{1,0:T(8,128)S(1)} collective-permute-done((f32[32,224]{1,0:T(8,128)S(1)}, f32[32,224]{1,0:T(8,128)S(1)}, u32[]{:S(2)}, u32[]{:S(2)}) %collective-permute-start.12) | collective-permute-done | bytes 28704 | tf_op jit(solution)/shard_map/ppermute | solution.py:285
  86.2 9.9 %collective-permute-start.13 = (f32[32,224]{1,0:T(8,128)S(1)}, f32[32,224]{1,0:T(8,128)S(1)}, u32[]{:S(2)}, u32[]{:S(2)}) collective-permute-start(f32[32,224]{1,0:T(8,128)S(1)} %get-tuple-element.63), channel_id=1, source_target_pairs={{0,504},{1,505},{2,506},{3,507},{4,508},{5,509},{6,510},{7,511},{2... | collective-permute-start | bytes 86024 | tf_op jit(solution)/shard_map/ppermute | solution.py:282
  96.2 1.3 %collective-permute-start.15 = (f32[32,224]{1,0:T(8,128)S(1)}, f32[32,224]{1,0:T(8,128)S(1)}, u32[]{:S(2)}, u32[]{:S(2)}) collective-permute-start(f32[32,224]{1,0:T(8,128)S(1)} %get-tuple-element.64), channel_id=1, source_target_pairs={{0,8},{1,9},{2,10},{3,11},{4,12},{5,13},{6,14},{7,15},{8,16},{9,17... | collective-permute-start | bytes 86024 | tf_op jit(solution)/shard_map/ppermute | solution.py:282
  97.5 2.1 %collective-permute-done.13 = f32[32,224]{1,0:T(8,128)S(1)} collective-permute-done((f32[32,224]{1,0:T(8,128)S(1)}, f32[32,224]{1,0:T(8,128)S(1)}, u32[]{:S(2)}, u32[]{:S(2)}) %collective-permute-start.13) | collective-permute-done | bytes 28704 | tf_op jit(solution)/shard_map/ppermute | solution.py:282
  (36 shorter events, 7.2 us)
Async XLA Ops:
  0.8 1.0 %copy-start.4 = (bf16[224,1024]{1,0:T(8,128)(2,1)S(1)}, bf16[224,1024]{1,0:T(8,128)(2,1)}, u32[]{:S(2)}) copy-start(bf16[224,1024]{1,0:T(8,128)(2,1)} %spectra_ref.1) | copy-start | bytes 1376260
  1.9 21.8 %collective-permute-start.1 = (bf16[240,1024]{1,0:T(8,128)(2,1)S(1)}, bf16[240,1024]{1,0:T(8,128)(2,1)S(1)}, u32[]{:S(2)}, u32[]{:S(2)}) collective-permute-start(bf16[240,1024]{1,0:T(8,128)(2,1)S(1)} %shard_map.28.zero_ref.refs_0_), channel_id=1, source_target_pairs={{4,0},{5,1},{6,2},{7,3},{8,4},{9,5},{10,6},{11,7},{12,8},{13,9},{1... | collective-permute-start | bytes 1474568 | tf_op jit(solution)/shard_map/ppermute | solution.py:279
  3.2 22.6 %collective-permute-start.6 = (bf16[240,1024]{1,0:T(8,128)(2,1)S(1)}, bf16[240,1024]{1,0:T(8,128)(2,1)S(1)}, u32[]{:S(2)}, u32[]{:S(2)}) collective-permute-start(bf16[240,1024]{1,0:T(8,128)(2,1)S(1)} %shard_map.28.zero_ref.refs_0_), channel_id=1, source_target_pairs={{0,4},{1,5},{2,6},{3,7},{4,8},{5,9},{6,10},{7,11},{8,12},{9,13},{1... | collective-permute-start | bytes 1474568 | tf_op jit(solution)/shard_map/ppermute | solution.py:279
  8.2 36.8 %collective-permute-start = (bf16[240,1024]{1,0:T(8,128)(2,1)S(1)}, bf16[240,1024]{1,0:T(8,128)(2,1)S(1)}, u32[]{:S(2)}, u32[]{:S(2)}) collective-permute-start(bf16[240,1024]{1,0:T(8,128)(2,1)S(1)} %shard_map.28.zero_ref.refs_0_), channel_id=1, source_target_pairs={{504,0},{505,1},{506,2},{507,3},{508,4},{509,5},{510,6},{511,7},{3... | collective-permute-start | bytes 1474568 | tf_op jit(solution)/shard_map/ppermute | solution.py:279
  23.8 21.2 %collective-permute-start.2 = (bf16[240,1024]{1,0:T(8,128)(2,1)S(1)}, bf16[240,1024]{1,0:T(8,128)(2,1)S(1)}, u32[]{:S(2)}, u32[]{:S(2)}) collective-permute-start(bf16[240,1024]{1,0:T(8,128)(2,1)S(1)} %collective-permute-done.1.other_ref), channel_id=1, source_target_pairs={{4,0},{5,1},{6,2},{7,3},{8,4},{9,5},{10,6},{11,7},{12,8},{13,9},{1... | collective-permute-start | bytes 1474568 | tf_op jit(solution)/shard_map/ppermute | solution.py:279
  25.1 0.8 copy-start
  25.9 19.2 %copy-start.2 = (bf16[240,1024]{1,0:T(8,128)(2,1)}, bf16[240,1024]{1,0:T(8,128)(2,1)S(1)}, u32[]{:S(2)}) copy-start(bf16[240,1024]{1,0:T(8,128)(2,1)S(1)} %collective-permute-done.6.other_ref) | copy-start | bytes 1474564
  25.9 22.6 %collective-permute-start.7 = (bf16[240,1024]{1,0:T(8,128)(2,1)S(1)}, bf16[240,1024]{1,0:T(8,128)(2,1)S(1)}, u32[]{:S(2)}, u32[]{:S(2)}) collective-permute-start(bf16[240,1024]{1,0:T(8,128)(2,1)S(1)} %collective-permute-done.6.other_ref), channel_id=1, source_target_pairs={{4,8},{5,9},{6,10},{7,11},{8,12},{9,13},{10,14},{11,15},{12,16},{1... | collective-permute-start | bytes 1474568 | tf_op jit(solution)/shard_map/ppermute | solution.py:279
  45.0 14.1 %collective-permute-start.3 = (bf16[240,1024]{1,0:T(8,128)(2,1)S(1)}, bf16[240,1024]{1,0:T(8,128)(2,1)S(1)}, u32[]{:S(2)}, u32[]{:S(2)}) collective-permute-start(bf16[240,1024]{1,0:T(8,128)(2,1)S(1)} %shard_map.29.up2_ref.refs_3_), channel_id=1, source_target_pairs={{0,2},{1,3},{2,0},{3,1},{4,6},{5,7},{6,4},{7,5},{8,10},{9,11},{10,... | collective-permute-start | bytes 1474568 | tf_op jit(solution)/shard_map/ppermute | solution.py:285
  49.3 14.0 %collective-permute-start.5 = (bf16[240,1024]{1,0:T(8,128)(2,1)}, bf16[240,1024]{1,0:T(8,128)(2,1)S(1)}, u32[]{:S(2)}, u32[]{:S(2)}) collective-permute-start(bf16[240,1024]{1,0:T(8,128)(2,1)} %get-tuple-element.66), channel_id=1, source_target_pairs={{4,0},{5,1},{6,2},{7,3},{24,28},{25,29},{26,30},{27,31},{36,32},{3... | collective-permute-start | bytes 1474568 | tf_op jit(solution)/shard_map/ppermute | solution.py:279
  50.6 14.8 %collective-permute-start.8 = (bf16[240,1024]{1,0:T(8,128)(2,1)S(1)}, bf16[240,1024]{1,0:T(8,128)(2,1)S(1)}, u32[]{:S(2)}, u32[]{:S(2)}) collective-permute-start(bf16[240,1024]{1,0:T(8,128)(2,1)S(1)} %shard_map.29.up2_ref.refs_3_), channel_id=1, source_target_pairs={{0,1},{1,0},{2,3},{3,2},{4,5},{5,4},{6,7},{7,6},{8,9},{9,8},{10,11... | collective-permute-start | bytes 1474568 | tf_op jit(solution)/shard_map/ppermute | solution.py:285
  59.2 11.6 %collective-permute-start.4 = (bf16[240,1024]{1,0:T(8,128)(2,1)S(1)}, bf16[240,1024]{1,0:T(8,128)(2,1)S(1)}, u32[]{:S(2)}, u32[]{:S(2)}) collective-permute-start(bf16[240,1024]{1,0:T(8,128)(2,1)S(1)} %collective-permute-done.3.extra_ref), channel_id=1, source_target_pairs={{0,1},{1,0},{2,3},{3,2},{4,5},{5,4},{6,7},{7,6},{8,9},{9,8},{10,11... | collective-permute-start | bytes 1474568 | tf_op jit(solution)/shard_map/ppermute | solution.py:285
  63.3 1.0 %copy-start.3 = (bf16[240,1024]{1,0:T(8,128)(2,1)S(1)}, bf16[240,1024]{1,0:T(8,128)(2,1)}, u32[]{:S(2)}) copy-start(bf16[240,1024]{1,0:T(8,128)(2,1)} %copy-done.2) | copy-start | bytes 1474564
  64.3 1.0 %copy-start.1 = (bf16[240,1024]{1,0:T(8,128)(2,1)S(1)}, bf16[240,1024]{1,0:T(8,128)(2,1)}, u32[]{:S(2)}) copy-start(bf16[240,1024]{1,0:T(8,128)(2,1)} %copy-done) | copy-start | bytes 1474564
  72.5 7.8 %collective-permute-start.11 = (f32[64,224]{1,0:T(8,128)S(1)}, f32[64,224]{1,0:T(8,128)S(1)}, u32[]{:S(2)}, u32[]{:S(2)}) collective-permute-start(f32[64,224]{1,0:T(8,128)S(1)} %pad_maximum_fusion.2), channel_id=1, source_target_pairs={{0,1},{1,0},{2,3},{3,2},{4,5},{5,4},{6,7},{7,6},{8,9},{9,8},{10,11... | collective-permute-start | bytes 172040 | tf_op jit(solution)/shard_map/ppermute | solution.py:285
  74.5 9.7 %collective-permute-start.10 = (f32[64,224]{1,0:T(8,128)S(1)}, f32[64,224]{1,0:T(8,128)S(1)}, u32[]{:S(2)}, u32[]{:S(2)}) collective-permute-start(f32[64,224]{1,0:T(8,128)S(1)} %pad_maximum_fusion.1), channel_id=1, source_target_pairs={{4,0},{5,1},{6,2},{7,3},{8,4},{9,5},{10,6},{11,7},{12,8},{13,9},{1... | collective-permute-start | bytes 172040 | tf_op jit(solution)/shard_map/ppermute | solution.py:282
  75.8 8.4 %collective-permute-start.9 = (f32[64,224]{1,0:T(8,128)S(1)}, f32[64,224]{1,0:T(8,128)S(1)}, u32[]{:S(2)}, u32[]{:S(2)}) collective-permute-start(f32[64,224]{1,0:T(8,128)S(1)} %pad_maximum_fusion), channel_id=1, source_target_pairs={{0,4},{1,5},{2,6},{3,7},{4,8},{5,9},{6,10},{7,11},{8,12},{9,13},{1... | collective-permute-start | bytes 172040 | tf_op jit(solution)/shard_map/ppermute | solution.py:282
  80.4 5.8 %collective-permute-start.12 = (f32[32,224]{1,0:T(8,128)S(1)}, f32[32,224]{1,0:T(8,128)S(1)}, u32[]{:S(2)}, u32[]{:S(2)}) collective-permute-start(f32[32,224]{1,0:T(8,128)S(1)} %slice_add_fusion.2), channel_id=1, source_target_pairs={{0,2},{1,3},{2,0},{3,1},{4,6},{5,7},{6,4},{7,5},{8,10},{9,11},{10,... | collective-permute-start | bytes 86024 | tf_op jit(solution)/shard_map/ppermute | solution.py:285
  82.9 14.5 %collective-permute-start.14 = (f32[32,224]{1,0:T(8,128)S(1)}, f32[32,224]{1,0:T(8,128)S(1)}, u32[]{:S(2)}, u32[]{:S(2)}) collective-permute-start(f32[32,224]{1,0:T(8,128)S(1)} %get-tuple-element.62), channel_id=1, source_target_pairs={{8,0},{9,1},{10,2},{11,3},{12,4},{13,5},{14,6},{15,7},{16,8},{17,9... | collective-permute-start | bytes 86024 | tf_op jit(solution)/shard_map/ppermute | solution.py:282
  86.2 13.4 %collective-permute-start.13 = (f32[32,224]{1,0:T(8,128)S(1)}, f32[32,224]{1,0:T(8,128)S(1)}, u32[]{:S(2)}, u32[]{:S(2)}) collective-permute-start(f32[32,224]{1,0:T(8,128)S(1)} %get-tuple-element.63), channel_id=1, source_target_pairs={{0,504},{1,505},{2,506},{3,507},{4,508},{5,509},{6,510},{7,511},{2... | collective-permute-start | bytes 86024 | tf_op jit(solution)/shard_map/ppermute | solution.py:282
  96.2 3.4 %collective-permute-start.15 = (f32[32,224]{1,0:T(8,128)S(1)}, f32[32,224]{1,0:T(8,128)S(1)}, u32[]{:S(2)}, u32[]{:S(2)}) collective-permute-start(f32[32,224]{1,0:T(8,128)S(1)} %get-tuple-element.64), channel_id=1, source_target_pairs={{0,8},{1,9},{2,10},{3,11},{4,12},{5,13},{6,14},{7,15},{8,16},{9,17... | collective-permute-start | bytes 86024 | tf_op jit(solution)/shard_map/ppermute | solution.py:282
where the time goes:
time: 101 us; the launch traced here: 100 us
  starting transfers between devices  55.1 us (55%)
  waiting for transfers between devices  31.4 us (31%)
  Pallas kernels  7.19 us (7%)
  local copies, waits for them, and re-layouts  4.66 us (5%)
  other arithmetic  1.59 us (2%)
    ppermute x6, starting transfers between devices, route(): return lax.ppermute(block, AXES, sources(source_of, n, column))  25 us
    ppermute x6, waiting for transfers between devices, route(): return lax.ppermute(block, AXES, sources(source_of, n, column))  20.6 us
    ppermute x5, starting transfers between devices, send(): lax.ppermute(block, AXES, [(i, source) for source, i in sources(source_of...  18.4 us
    ppermute x5, starting transfers between devices, swap(): return lax.ppermute(block, AXES, [(i, i ^ bits) for i in range(n)])  11.7 us
    ppermute x5, waiting for transfers between devices, swap(): return lax.ppermute(block, AXES, [(i, i ^ bits) for i in range(n)])  8.6 us
    unnamed x11, local copies, waits for them, and re-layouts  4.66 us
    pallas_call x2, Pallas kernels, extra_pairs(): pl.pallas_call(extra_body, out_shape=[total] * 6, in_specs=[pl.BlockSpec(...  3.45 us
    ppermute x5, waiting for transfers between devices, send(): lax.ppermute(block, AXES, [(i, source) for source, i in sources(source_of...  2.14 us
  transfers between devices with their start and end apart: 16, of which 5 were waited for; matrix products, arithmetic and copies ran while one was open for 1% of the time, Pallas kernels for 5%

commit v1 on v0

--- a/solution.py
+++ b/solution.py
@@ -298,8 +298,8 @@
     up2, down2 = lax.optimization_barrier((up2, down2))
     down2 = jnp.where(low, far, down2)
     back, _, _ = lax.optimization_barrier((back, up2, down2))
-    up = pick(level == column - 1, back, up)
-    down = pick(level == 0, back, down)
+    up = jnp.where(level == column - 1, back, up)
+    down = jnp.where(level == 0, back, down)
 
     total, two, eight, for_sibling, zero_norms, up2_norms, down2_norms = early_pairs(
         (me & 1) == 0, [sibling, zero, up2, down2]
@@ -333,7 +333,7 @@
     crossing = jnp.where(high, two + downward[COLS:], eight + upward[COLS:])
     far_sums = send(eight, lambda i, column, quads: inner_source(i, -2, column, quads))
     far_sums = far_sums + send(two, lambda i, column, quads: inner_source(i, 2, column, quads))
-    total = total + send(crossing, far_source) + far_sums
+    total = total + far_sums + send(crossing, far_source)
     return total.T
 
 

time: 101 us -> 100 us (0.990)
  local copies, waits for them, and re-layouts: 4.66 us -> 1.87 us
  starting transfers between devices: 55.1 us -> 56.6 us
  other arithmetic: 1.59 us -> 2.73 us
    unnamed x11 -> x7, local copies, waits for them, and re-layouts: 4.66 us -> 1.87 us
    select_n x0 -> x1, other arithmetic: none -> 1.13 us  [on_device(): down = jnp.where(level == 0, back, down)]
    ppermute x5, waiting for transfers between devices: 8.6 us -> 7.56 us  [swap(): return lax.ppermute(block, AXES, [(i, i ^ bits) for i in range(n)])]
  transfers between devices with their start and end apart: 16 -> 16, of which waited for: 5 -> 7; matrix products, arithmetic and copies ran while one was open for 1% -> 2% of each run, Pallas kernels for 5% -> 5%
where the time goes in v1:
time: 100 us; the launch traced here: 99.5 us
  starting transfers between devices  56.6 us (57%)
  waiting for transfers between devices  31 us (31%)
  Pallas kernels  7.1 us (7%)
  other arithmetic  2.73 us (3%)
  local copies, waits for them, and re-layouts  1.87 us (2%)
    ppermute x6, starting transfers between devices, route(): return lax.ppermute(block, AXES, sources(source_of, n, column))  25.8 us
    ppermute x6, waiting for transfers between devices, route(): return lax.ppermute(block, AXES, sources(source_of, n, column))  20.8 us
    ppermute x5, starting transfers between devices, send(): lax.ppermute(block, AXES, [(i, source) for source, i in sources(source_of...  19.1 us
    ppermute x5, starting transfers between devices, swap(): return lax.ppermute(block, AXES, [(i, i ^ bits) for i in range(n)])  11.7 us
    ppermute x5, waiting for transfers between devices, swap(): return lax.ppermute(block, AXES, [(i, i ^ bits) for i in range(n)])  7.56 us
    pallas_call x2, Pallas kernels, extra_pairs(): pl.pallas_call(extra_body, out_shape=[total] * 6, in_specs=[pl.BlockSpec(...  3.45 us
    ppermute x5, waiting for transfers between devices, send(): lax.ppermute(block, AXES, [(i, source) for source, i in sources(source_of...  2.62 us
  transfers between devices with their start and end apart: 16, of which 7 were waited for; matrix products, arithmetic and copies ran while one was open for 2% of the time, Pallas kernels for 5%

profile of v1, /device:TPU:8, one launch (start us, length us, event | category | flops | bytes accessed | tf_op | source)
XLA Modules:
  0.0 99.5 jit_solution(129873369749677978)
XLA Ops:
  1.9 1.3 %collective-permute-start.1 = (bf16[240,1024]{1,0:T(8,128)(2,1)S(1)}, bf16[240,1024]{1,0:T(8,128)(2,1)S(1)}, u32[]{:S(2)}, u32[]{:S(2)}) collective-permute-start(bf16[240,1024]{1,0:T(8,128)(2,1)S(1)} %shard_map.28.zero_ref.refs_0_), channel_id=1, source_target_pairs={{4,0},{5,1},{6,2},{7,3},{8,4},{9,5},{10,6},{11,7},{12,8},{13,9},{1... | collective-permute-start | bytes 1474568 | tf_op jit(solution)/shard_map/ppermute | solution.py:279
  3.2 4.9 %collective-permute-start.6 = (bf16[240,1024]{1,0:T(8,128)(2,1)S(1)}, bf16[240,1024]{1,0:T(8,128)(2,1)S(1)}, u32[]{:S(2)}, u32[]{:S(2)}) collective-permute-start(bf16[240,1024]{1,0:T(8,128)(2,1)S(1)} %shard_map.28.zero_ref.refs_0_), channel_id=1, source_target_pairs={{0,4},{1,5},{2,6},{3,7},{4,8},{5,9},{6,10},{7,11},{8,12},{9,13},{1... | collective-permute-start | bytes 1474568 | tf_op jit(solution)/shard_map/ppermute | solution.py:279
  8.2 15.6 %collective-permute-start = (bf16[240,1024]{1,0:T(8,128)(2,1)S(1)}, bf16[240,1024]{1,0:T(8,128)(2,1)S(1)}, u32[]{:S(2)}, u32[]{:S(2)}) collective-permute-start(bf16[240,1024]{1,0:T(8,128)(2,1)S(1)} %shard_map.28.zero_ref.refs_0_), channel_id=1, source_target_pairs={{504,0},{505,1},{506,2},{507,3},{508,4},{509,5},{510,6},{511,7},{3... | collective-permute-start | bytes 1474568 | tf_op jit(solution)/shard_map/ppermute | solution.py:279
  23.8 1.3 %collective-permute-start.2 = (bf16[240,1024]{1,0:T(8,128)(2,1)S(1)}, bf16[240,1024]{1,0:T(8,128)(2,1)S(1)}, u32[]{:S(2)}, u32[]{:S(2)}) collective-permute-start(bf16[240,1024]{1,0:T(8,128)(2,1)S(1)} %collective-permute-done.1), channel_id=1, source_target_pairs={{4,0},{5,1},{6,2},{7,3},{8,4},{9,5},{10,6},{11,7},{12,8},{13,9},{1... | collective-permute-start | bytes 1474568 | tf_op jit(solution)/shard_map/ppermute | solution.py:279
  25.1 1.4 %collective-permute-start.7 = (bf16[240,1024]{1,0:T(8,128)(2,1)S(1)}, bf16[240,1024]{1,0:T(8,128)(2,1)}, u32[]{:S(2)}, u32[]{:S(2)}) collective-permute-start(bf16[240,1024]{1,0:T(8,128)(2,1)S(1)} %collective-permute-done.6), channel_id=1, source_target_pairs={{4,8},{5,9},{6,10},{7,11},{8,12},{9,13},{10,14},{11,15},{12,16},{1... | collective-permute-start | bytes 1474568 | tf_op jit(solution)/shard_map/ppermute | solution.py:279
  26.5 18.5 %collective-permute-done.one_ref = bf16[240,1024]{1,0:T(8,128)(2,1)S(1)} collective-permute-done((bf16[240,1024]{1,0:T(8,128)(2,1)S(1)}, bf16[240,1024]{1,0:T(8,128)(2,1)S(1)}, u32[]{:S(2)}, u32[]{:S(2)}) %collective-permute-start) | collective-permute-done | bytes 491552 | tf_op jit(solution)/shard_map/ppermute | solution.py:279
  45.0 3.4 %collective-permute-start.3 = (bf16[240,1024]{1,0:T(8,128)(2,1)S(1)}, bf16[240,1024]{1,0:T(8,128)(2,1)S(1)}, u32[]{:S(2)}, u32[]{:S(2)}) collective-permute-start(bf16[240,1024]{1,0:T(8,128)(2,1)S(1)} %shard_map.29.up2_ref.refs_3_), channel_id=1, source_target_pairs={{0,2},{1,3},{2,0},{3,1},{4,6},{5,7},{6,4},{7,5},{8,10},{9,11},{10,... | collective-permute-start | bytes 1474568 | tf_op jit(solution)/shard_map/ppermute | solution.py:285
  49.3 1.3 %collective-permute-start.5 = (bf16[240,1024]{1,0:T(8,128)(2,1)}, bf16[240,1024]{1,0:T(8,128)(2,1)}, u32[]{:S(2)}, u32[]{:S(2)}) collective-permute-start(bf16[240,1024]{1,0:T(8,128)(2,1)} %get-tuple-element.68), channel_id=1, source_target_pairs={{4,0},{5,1},{6,2},{7,3},{24,28},{25,29},{26,30},{27,31},{36,32},{3... | collective-permute-start | bytes 1474568 | tf_op jit(solution)/shard_map/ppermute | solution.py:279
  50.6 1.9 %collective-permute-start.8 = (bf16[240,1024]{1,0:T(8,128)(2,1)S(1)}, bf16[240,1024]{1,0:T(8,128)(2,1)S(1)}, u32[]{:S(2)}, u32[]{:S(2)}) collective-permute-start(bf16[240,1024]{1,0:T(8,128)(2,1)S(1)} %shard_map.29.up2_ref.refs_3_), channel_id=1, source_target_pairs={{0,1},{1,0},{2,3},{3,2},{4,5},{5,4},{6,7},{7,6},{8,9},{9,8},{10,11... | collective-permute-start | bytes 1474568 | tf_op jit(solution)/shard_map/ppermute | solution.py:285
  52.5 6.6 %collective-permute-done.3.extra_ref = bf16[240,1024]{1,0:T(8,128)(2,1)S(1)} collective-permute-done((bf16[240,1024]{1,0:T(8,128)(2,1)S(1)}, bf16[240,1024]{1,0:T(8,128)(2,1)S(1)}, u32[]{:S(2)}, u32[]{:S(2)}) %collective-permute-start.3) | collective-permute-done | bytes 491552 | tf_op jit(solution)/shard_map/ppermute | solution.py:285
  59.2 1.9 %collective-permute-start.4 = (bf16[240,1024]{1,0:T(8,128)(2,1)S(1)}, bf16[240,1024]{1,0:T(8,128)(2,1)S(1)}, u32[]{:S(2)}, u32[]{:S(2)}) collective-permute-start(bf16[240,1024]{1,0:T(8,128)(2,1)S(1)} %collective-permute-done.3.extra_ref), channel_id=1, source_target_pairs={{0,1},{1,0},{2,3},{3,2},{4,5},{5,4},{6,7},{7,6},{8,9},{9,8},{10,11... | collective-permute-start | bytes 1474568 | tf_op jit(solution)/shard_map/ppermute | solution.py:285
  61.1 2.3 %collective-permute-done.5 = bf16[240,1024]{1,0:T(8,128)(2,1)} collective-permute-done((bf16[240,1024]{1,0:T(8,128)(2,1)}, bf16[240,1024]{1,0:T(8,128)(2,1)}, u32[]{:S(2)}, u32[]{:S(2)}) %collective-permute-start.5) | collective-permute-done | bytes 491552 | tf_op jit(solution)/shard_map/ppermute | solution.py:279
  63.4 1.6 %shard_map.30 = (f32[32,224]{1,0:T(8,128)S(1)}, f32[32,224]{1,0:T(8,128)S(1)}, f32[32,224]{1,0:T(8,128)S(1)}, f32[32,224]{1,0:T(8,128)S(1)}, f32[1,224]{1,0:T(1,...) custom-call(s32[1]{0:T(128)} %bitcast.2.low_ref, bf16[240,1024]{1,0:T(8,128)(2,1)S(1)} %collective-permute-done.8.extra_ref.refs_4_, ...), custom_call_target="tpu_custom_call" | custom-call | flops 436731904 | bytes 1966080 | tf_op jit(solution)/shard_map/pallas_call | solution.py:260
  65.0 1.1 %broadcast_select_fusion = (bf16[240,1024]{1,0:T(8,128)(2,1)S(1)}, bf16[240,1024]{1,0:T(8,128)(2,1)S(1)}) fusion(bf16[240,1024]{1,0:T(8,128)(2,1)} %collective-permute-done.5, bf16[240,1024]{1,0:T(8,128)(2,1)S(1)} %copy-done.2, pred[]{:T(512)S(6)} %eq.28, bf16[240,1024]{1,0:T(8,128)(2,1)S(1)} %collective-permute-done.1, pred[]{:T(512)S(6)} %eq.25), kind=kLoop, calls=%fused_computation | loop fusion | flops 491520 | bytes 2457602 | tf_op jit(solution)/shard_map/jit(_where)/select_n | solution.py:302
  66.1 2.0 %shard_map.31 = (f32[32,224]{1,0:T(8,128)S(1)}, f32[32,224]{1,0:T(8,128)S(1)}, f32[32,224]{1,0:T(8,128)S(1)}, f32[32,224]{1,0:T(8,128)S(1)}, f32[32,224]{1,0:T(8...) custom-call(bf16[240,1024]{1,0:T(8,128)(2,1)S(1)} %shard_map.28.zero_ref.refs_0_, ...), custom_call_target="tpu_custom_call" | custom-call | flops 545914880 | bytes 2457600 | tf_op jit(solution)/shard_map/pallas_call | solution.py:174
  68.1 1.7 %shard_map.32 = (f32[32,224]{1,0:T(8,128)S(1)}, f32[32,224]{1,0:T(8,128)S(1)}, f32[32,224]{1,0:T(8,128)S(1)}, f32[32,224]{1,0:T(8,128)S(1)}, f32[32,224]{1,0:T(8,128)S(1)}, /*index=5*/f32[32,224]{1,0:T(8,128)S(1)}) custom-call(s32[1]{0:T(128)} %bitcast.low_ref, bf16[240,1024]{1,0:T(8,128)(2,1)S(1)} %collective-permute-done.3.extra_ref, ...), custom_call_target="tpu_custom_call" | custom-call | flops 436731904 | bytes 2949120 | tf_op jit(solution)/shard_map/pallas_call | solution.py:215
  69.9 1.7 %shard_map.33 = (f32[32,224]{1,0:T(8,128)S(1)}, f32[32,224]{1,0:T(8,128)S(1)}, f32[32,224]{1,0:T(8,128)S(1)}, f32[32,224]{1,0:T(8,128)S(1)}, f32[32,224]{1,0:T(8,128)S(1)}, /*index=5*/f32[32,224]{1,0:T(8,128)S(1)}) custom-call(s32[1]{0:T(128)} %bitcast.low_ref, bf16[240,1024]{1,0:T(8,128)(2,1)S(1)} %collective-permute-done.4.extra_ref, ...), custom_call_target="tpu_custom_call" | custom-call | flops 436731904 | bytes 2949120 | tf_op jit(solution)/shard_map/pallas_call | solution.py:215
  71.7 1.9 %collective-permute-start.12 = (f32[64,224]{1,0:T(8,128)S(1)}, f32[64,224]{1,0:T(8,128)S(1)}, u32[]{:S(2)}, u32[]{:S(2)}) collective-permute-start(f32[64,224]{1,0:T(8,128)S(1)} %pad_maximum_fusion.2), channel_id=1, source_target_pairs={{0,1},{1,0},{2,3},{3,2},{4,5},{5,4},{6,7},{7,6},{8,9},{9,8},{10,11... | collective-permute-start | bytes 172040 | tf_op jit(solution)/shard_map/ppermute | solution.py:285
  73.6 1.5 %collective-permute-start.9 = (f32[64,224]{1,0:T(8,128)S(1)}, f32[64,224]{1,0:T(8,128)S(1)}, u32[]{:S(2)}, u32[]{:S(2)}) collective-permute-start(f32[64,224]{1,0:T(8,128)S(1)} %pad_maximum_fusion), channel_id=1, source_target_pairs={{0,4},{1,5},{2,6},{3,7},{4,8},{5,9},{6,10},{7,11},{8,12},{9,13},{1... | collective-permute-start | bytes 172040 | tf_op jit(solution)/shard_map/ppermute | solution.py:282
  75.1 1.3 %collective-permute-start.10 = (f32[64,224]{1,0:T(8,128)S(1)}, f32[64,224]{1,0:T(8,128)S(1)}, u32[]{:S(2)}, u32[]{:S(2)}) collective-permute-start(f32[64,224]{1,0:T(8,128)S(1)} %pad_maximum_fusion.1), channel_id=1, source_target_pairs={{4,0},{5,1},{6,2},{7,3},{8,4},{9,5},{10,6},{11,7},{12,8},{13,9},{1... | collective-permute-start | bytes 172040 | tf_op jit(solution)/shard_map/ppermute | solution.py:282
  76.4 2.5 %collective-permute-start.13 = (f32[32,224]{1,0:T(8,128)S(1)}, f32[32,224]{1,0:T(8,128)S(1)}, u32[]{:S(2)}, u32[]{:S(2)}) collective-permute-start(f32[32,224]{1,0:T(8,128)S(1)} %slice_add_fusion.2), channel_id=1, source_target_pairs={{0,2},{1,3},{2,0},{3,1},{4,6},{5,7},{6,4},{7,5},{8,10},{9,11},{10,... | collective-permute-start | bytes 86024 | tf_op jit(solution)/shard_map/ppermute | solution.py:285
  79.0 1.3 %collective-permute-start.11 = (f32[32,224]{1,0:T(8,128)S(1)}, f32[32,224]{1,0:T(8,128)S(1)}, u32[]{:S(2)}, u32[]{:S(2)}) collective-permute-start(f32[32,224]{1,0:T(8,128)S(1)} %get-tuple-element.58), channel_id=1, source_target_pairs={{8,0},{9,1},{10,2},{11,3},{12,4},{13,5},{14,6},{15,7},{16,8},{17,9... | collective-permute-start | bytes 86024 | tf_op jit(solution)/shard_map/ppermute | solution.py:282
  82.2 13.7 %collective-permute-start.15 = (f32[32,224]{1,0:T(8,128)S(1)}, f32[32,224]{1,0:T(8,128)S(1)}, u32[]{:S(2)}, u32[]{:S(2)}) collective-permute-start(f32[32,224]{1,0:T(8,128)S(1)} %get-tuple-element.63), channel_id=1, source_target_pairs={{0,504},{1,505},{2,506},{3,507},{4,508},{5,509},{6,510},{7,511},{2... | collective-permute-start | bytes 86024 | tf_op jit(solution)/shard_map/ppermute | solution.py:282
  96.0 1.3 %collective-permute-start.14 = (f32[32,224]{1,0:T(8,128)S(1)}, f32[32,224]{1,0:T(8,128)S(1)}, u32[]{:S(2)}, u32[]{:S(2)}) collective-permute-start(f32[32,224]{1,0:T(8,128)S(1)} %get-tuple-element.64), channel_id=1, source_target_pairs={{0,8},{1,9},{2,10},{3,11},{4,12},{5,13},{6,14},{7,15},{8,16},{9,17... | collective-permute-start | bytes 86024 | tf_op jit(solution)/shard_map/ppermute | solution.py:282
  (31 shorter events, 7.1 us)
Async XLA Ops:
  0.8 1.0 %copy-start = (bf16[224,1024]{1,0:T(8,128)(2,1)S(1)}, bf16[224,1024]{1,0:T(8,128)(2,1)}, u32[]{:S(2)}) copy-start(bf16[224,1024]{1,0:T(8,128)(2,1)} %spectra_ref.1) | copy-start | bytes 1376260
  1.9 21.8 %collective-permute-start.1 = (bf16[240,1024]{1,0:T(8,128)(2,1)S(1)}, bf16[240,1024]{1,0:T(8,128)(2,1)S(1)}, u32[]{:S(2)}, u32[]{:S(2)}) collective-permute-start(bf16[240,1024]{1,0:T(8,128)(2,1)S(1)} %shard_map.28.zero_ref.refs_0_), channel_id=1, source_target_pairs={{4,0},{5,1},{6,2},{7,3},{8,4},{9,5},{10,6},{11,7},{12,8},{13,9},{1... | collective-permute-start | bytes 1474568 | tf_op jit(solution)/shard_map/ppermute | solution.py:279
  3.2 21.8 %collective-permute-start.6 = (bf16[240,1024]{1,0:T(8,128)(2,1)S(1)}, bf16[240,1024]{1,0:T(8,128)(2,1)S(1)}, u32[]{:S(2)}, u32[]{:S(2)}) collective-permute-start(bf16[240,1024]{1,0:T(8,128)(2,1)S(1)} %shard_map.28.zero_ref.refs_0_), channel_id=1, source_target_pairs={{0,4},{1,5},{2,6},{3,7},{4,8},{5,9},{6,10},{7,11},{8,12},{9,13},{1... | collective-permute-start | bytes 1474568 | tf_op jit(solution)/shard_map/ppermute | solution.py:279
  8.2 36.8 %collective-permute-start = (bf16[240,1024]{1,0:T(8,128)(2,1)S(1)}, bf16[240,1024]{1,0:T(8,128)(2,1)S(1)}, u32[]{:S(2)}, u32[]{:S(2)}) collective-permute-start(bf16[240,1024]{1,0:T(8,128)(2,1)S(1)} %shard_map.28.zero_ref.refs_0_), channel_id=1, source_target_pairs={{504,0},{505,1},{506,2},{507,3},{508,4},{509,5},{510,6},{511,7},{3... | collective-permute-start | bytes 1474568 | tf_op jit(solution)/shard_map/ppermute | solution.py:279
  23.8 21.2 %collective-permute-start.2 = (bf16[240,1024]{1,0:T(8,128)(2,1)S(1)}, bf16[240,1024]{1,0:T(8,128)(2,1)S(1)}, u32[]{:S(2)}, u32[]{:S(2)}) collective-permute-start(bf16[240,1024]{1,0:T(8,128)(2,1)S(1)} %collective-permute-done.1), channel_id=1, source_target_pairs={{4,0},{5,1},{6,2},{7,3},{8,4},{9,5},{10,6},{11,7},{12,8},{13,9},{1... | collective-permute-start | bytes 1474568 | tf_op jit(solution)/shard_map/ppermute | solution.py:279
  25.1 20.0 %copy-start.1 = (bf16[240,1024]{1,0:T(8,128)(2,1)}, bf16[240,1024]{1,0:T(8,128)(2,1)S(1)}, u32[]{:S(2)}) copy-start(bf16[240,1024]{1,0:T(8,128)(2,1)S(1)} %collective-permute-done.6) | copy-start | bytes 1474564
  25.1 23.4 %collective-permute-start.7 = (bf16[240,1024]{1,0:T(8,128)(2,1)S(1)}, bf16[240,1024]{1,0:T(8,128)(2,1)}, u32[]{:S(2)}, u32[]{:S(2)}) collective-permute-start(bf16[240,1024]{1,0:T(8,128)(2,1)S(1)} %collective-permute-done.6), channel_id=1, source_target_pairs={{4,8},{5,9},{6,10},{7,11},{8,12},{9,13},{10,14},{11,15},{12,16},{1... | collective-permute-start | bytes 1474568 | tf_op jit(solution)/shard_map/ppermute | solution.py:279
  45.0 14.1 %collective-permute-start.3 = (bf16[240,1024]{1,0:T(8,128)(2,1)S(1)}, bf16[240,1024]{1,0:T(8,128)(2,1)S(1)}, u32[]{:S(2)}, u32[]{:S(2)}) collective-permute-start(bf16[240,1024]{1,0:T(8,128)(2,1)S(1)} %shard_map.29.up2_ref.refs_3_), channel_id=1, source_target_pairs={{0,2},{1,3},{2,0},{3,1},{4,6},{5,7},{6,4},{7,5},{8,10},{9,11},{10,... | collective-permute-start | bytes 1474568 | tf_op jit(solution)/shard_map/ppermute | solution.py:285
  49.3 14.1 %collective-permute-start.5 = (bf16[240,1024]{1,0:T(8,128)(2,1)}, bf16[240,1024]{1,0:T(8,128)(2,1)}, u32[]{:S(2)}, u32[]{:S(2)}) collective-permute-start(bf16[240,1024]{1,0:T(8,128)(2,1)} %get-tuple-element.68), channel_id=1, source_target_pairs={{4,0},{5,1},{6,2},{7,3},{24,28},{25,29},{26,30},{27,31},{36,32},{3... | collective-permute-start | bytes 1474568 | tf_op jit(solution)/shard_map/ppermute | solution.py:279
  50.6 12.8 %collective-permute-start.8 = (bf16[240,1024]{1,0:T(8,128)(2,1)S(1)}, bf16[240,1024]{1,0:T(8,128)(2,1)S(1)}, u32[]{:S(2)}, u32[]{:S(2)}) collective-permute-start(bf16[240,1024]{1,0:T(8,128)(2,1)S(1)} %shard_map.29.up2_ref.refs_3_), channel_id=1, source_target_pairs={{0,1},{1,0},{2,3},{3,2},{4,5},{5,4},{6,7},{7,6},{8,9},{9,8},{10,11... | collective-permute-start | bytes 1474568 | tf_op jit(solution)/shard_map/ppermute | solution.py:285
  59.2 10.7 %collective-permute-start.4 = (bf16[240,1024]{1,0:T(8,128)(2,1)S(1)}, bf16[240,1024]{1,0:T(8,128)(2,1)S(1)}, u32[]{:S(2)}, u32[]{:S(2)}) collective-permute-start(bf16[240,1024]{1,0:T(8,128)(2,1)S(1)} %collective-permute-done.3.extra_ref), channel_id=1, source_target_pairs={{0,1},{1,0},{2,3},{3,2},{4,5},{5,4},{6,7},{7,6},{8,9},{9,8},{10,11... | collective-permute-start | bytes 1474568 | tf_op jit(solution)/shard_map/ppermute | solution.py:285
  63.4 1.6 %copy-start.2 = (bf16[240,1024]{1,0:T(8,128)(2,1)S(1)}, bf16[240,1024]{1,0:T(8,128)(2,1)}, u32[]{:S(2)}) copy-start(bf16[240,1024]{1,0:T(8,128)(2,1)} %copy-done.1) | copy-start | bytes 1474564
  71.7 4.7 %collective-permute-start.12 = (f32[64,224]{1,0:T(8,128)S(1)}, f32[64,224]{1,0:T(8,128)S(1)}, u32[]{:S(2)}, u32[]{:S(2)}) collective-permute-start(f32[64,224]{1,0:T(8,128)S(1)} %pad_maximum_fusion.2), channel_id=1, source_target_pairs={{0,1},{1,0},{2,3},{3,2},{4,5},{5,4},{6,7},{7,6},{8,9},{9,8},{10,11... | collective-permute-start | bytes 172040 | tf_op jit(solution)/shard_map/ppermute | solution.py:285
  73.6 6.6 %collective-permute-start.9 = (f32[64,224]{1,0:T(8,128)S(1)}, f32[64,224]{1,0:T(8,128)S(1)}, u32[]{:S(2)}, u32[]{:S(2)}) collective-permute-start(f32[64,224]{1,0:T(8,128)S(1)} %pad_maximum_fusion), channel_id=1, source_target_pairs={{0,4},{1,5},{2,6},{3,7},{4,8},{5,9},{6,10},{7,11},{8,12},{9,13},{1... | collective-permute-start | bytes 172040 | tf_op jit(solution)/shard_map/ppermute | solution.py:282
  75.1 6.2 %collective-permute-start.10 = (f32[64,224]{1,0:T(8,128)S(1)}, f32[64,224]{1,0:T(8,128)S(1)}, u32[]{:S(2)}, u32[]{:S(2)}) collective-permute-start(f32[64,224]{1,0:T(8,128)S(1)} %pad_maximum_fusion.1), channel_id=1, source_target_pairs={{4,0},{5,1},{6,2},{7,3},{8,4},{9,5},{10,6},{11,7},{12,8},{13,9},{1... | collective-permute-start | bytes 172040 | tf_op jit(solution)/shard_map/ppermute | solution.py:282
  76.4 5.8 %collective-permute-start.13 = (f32[32,224]{1,0:T(8,128)S(1)}, f32[32,224]{1,0:T(8,128)S(1)}, u32[]{:S(2)}, u32[]{:S(2)}) collective-permute-start(f32[32,224]{1,0:T(8,128)S(1)} %slice_add_fusion.2), channel_id=1, source_target_pairs={{0,2},{1,3},{2,0},{3,1},{4,6},{5,7},{6,4},{7,5},{8,10},{9,11},{10,... | collective-permute-start | bytes 86024 | tf_op jit(solution)/shard_map/ppermute | solution.py:285
  79.0 18.3 %collective-permute-start.11 = (f32[32,224]{1,0:T(8,128)S(1)}, f32[32,224]{1,0:T(8,128)S(1)}, u32[]{:S(2)}, u32[]{:S(2)}) collective-permute-start(f32[32,224]{1,0:T(8,128)S(1)} %get-tuple-element.58), channel_id=1, source_target_pairs={{8,0},{9,1},{10,2},{11,3},{12,4},{13,5},{14,6},{15,7},{16,8},{17,9... | collective-permute-start | bytes 86024 | tf_op jit(solution)/shard_map/ppermute | solution.py:282
  82.2 15.8 %collective-permute-start.15 = (f32[32,224]{1,0:T(8,128)S(1)}, f32[32,224]{1,0:T(8,128)S(1)}, u32[]{:S(2)}, u32[]{:S(2)}) collective-permute-start(f32[32,224]{1,0:T(8,128)S(1)} %get-tuple-element.63), channel_id=1, source_target_pairs={{0,504},{1,505},{2,506},{3,507},{4,508},{5,509},{6,510},{7,511},{2... | collective-permute-start | bytes 86024 | tf_op jit(solution)/shard_map/ppermute | solution.py:282
  96.0 2.9 %collective-permute-start.14 = (f32[32,224]{1,0:T(8,128)S(1)}, f32[32,224]{1,0:T(8,128)S(1)}, u32[]{:S(2)}, u32[]{:S(2)}) collective-permute-start(f32[32,224]{1,0:T(8,128)S(1)} %get-tuple-element.64), channel_id=1, source_target_pairs={{0,8},{1,9},{2,10},{3,11},{4,12},{5,13},{6,14},{7,15},{8,16},{9,17... | collective-permute-start | bytes 86024 | tf_op jit(solution)/shard_map/ppermute | solution.py:282

commit v2 on v1

--- a/solution.py
+++ b/solution.py
@@ -296,7 +296,7 @@
     sibling = swap(up2, 1)
     across = swap(beside, 1)
     up2, down2 = lax.optimization_barrier((up2, down2))
-    down2 = jnp.where(low, far, down2)
+    down2 = pick(low, far, down2)
     back, _, _ = lax.optimization_barrier((back, up2, down2))
     up = jnp.where(level == column - 1, back, up)
     down = jnp.where(level == 0, back, down)

time: 100 us -> 99.9 us (level)
  the two profiles are of different devices: /device:TPU:8 before, /device:TPU:128 now
where the time goes in v2:
time: 99.9 us; the launch traced here: 99.3 us
  starting transfers between devices  52.1 us (52%)
  waiting for transfers between devices  34.9 us (35%)
  Pallas kernels  7.16 us (7%)
  other arithmetic  2.88 us (3%)
  local copies, waits for them, and re-layouts  1.87 us (2%)
    ppermute x5, starting transfers between devices, send(): lax.ppermute(block, AXES, [(i, source) for source, i in sources(source_of...  23 us
    ppermute x6, waiting for transfers between devices, route(): return lax.ppermute(block, AXES, sources(source_of, n, column))  16.9 us
    ppermute x6, starting transfers between devices, route(): return lax.ppermute(block, AXES, sources(source_of, n, column))  16.1 us
    ppermute x5, starting transfers between devices, swap(): return lax.ppermute(block, AXES, [(i, i ^ bits) for i in range(n)])  13 us
    ppermute x5, waiting for transfers between devices, send(): lax.ppermute(block, AXES, [(i, source) for source, i in sources(source_of...  11.9 us
    ppermute x5, waiting for transfers between devices, swap(): return lax.ppermute(block, AXES, [(i, i ^ bits) for i in range(n)])  5.98 us
    pallas_call x2, Pallas kernels, extra_pairs(): pl.pallas_call(extra_body, out_shape=[total] * 6, in_specs=[pl.BlockSpec(...  3.45 us
  transfers between devices with their start and end apart: 16, of which 4 were waited for; matrix products, arithmetic and copies ran while one was open for 2% of the time, Pallas kernels for 5%

profile of v2, /device:TPU:128, one launch (start us, length us, event | category | flops | bytes accessed | tf_op | source)
XLA Modules:
  0.0 99.3 jit_solution(7310564288310337016)
XLA Ops:
  0.8 1.0 %copy-done = bf16[224,1024]{1,0:T(8,128)(2,1)S(1)} copy-done((bf16[224,1024]{1,0:T(8,128)(2,1)S(1)}, bf16[224,1024]{1,0:T(8,128)(2,1)}, u32[]{:S(2)}) %copy-start) | copy-done | bytes 458776
  1.9 1.9 %collective-permute-start.1 = (bf16[240,1024]{1,0:T(8,128)(2,1)S(1)}, bf16[240,1024]{1,0:T(8,128)(2,1)S(1)}, u32[]{:S(2)}, u32[]{:S(2)}) collective-permute-start(bf16[240,1024]{1,0:T(8,128)(2,1)S(1)} %shard_map.28.zero_ref.refs_0_), channel_id=1, source_target_pairs={{4,0},{5,1},{6,2},{7,3},{8,4},{9,5},{10,6},{11,7},{12,8},{13,9},{1... | collective-permute-start | bytes 1474568 | tf_op jit(solution)/shard_map/ppermute | solution.py:279
  3.9 4.3 %collective-permute-start.6 = (bf16[240,1024]{1,0:T(8,128)(2,1)S(1)}, bf16[240,1024]{1,0:T(8,128)(2,1)}, u32[]{:S(2)}, u32[]{:S(2)}) collective-permute-start(bf16[240,1024]{1,0:T(8,128)(2,1)S(1)} %shard_map.28.zero_ref.refs_0_), channel_id=1, source_target_pairs={{0,4},{1,5},{2,6},{3,7},{4,8},{5,9},{6,10},{7,11},{8,12},{9,13},{1... | collective-permute-start | bytes 1474568 | tf_op jit(solution)/shard_map/ppermute | solution.py:279
  8.8 8.6 %collective-permute-done.1 = bf16[240,1024]{1,0:T(8,128)(2,1)S(1)} collective-permute-done((bf16[240,1024]{1,0:T(8,128)(2,1)S(1)}, bf16[240,1024]{1,0:T(8,128)(2,1)S(1)}, u32[]{:S(2)}, u32[]{:S(2)}) %collective-permute-start.1) | collective-permute-done | bytes 491552 | tf_op jit(solution)/shard_map/ppermute | solution.py:279
  17.4 5.8 %collective-permute-start.2 = (bf16[240,1024]{1,0:T(8,128)(2,1)S(1)}, bf16[240,1024]{1,0:T(8,128)(2,1)S(1)}, u32[]{:S(2)}, u32[]{:S(2)}) collective-permute-start(bf16[240,1024]{1,0:T(8,128)(2,1)S(1)} %collective-permute-done.1), channel_id=1, source_target_pairs={{4,0},{5,1},{6,2},{7,3},{8,4},{9,5},{10,6},{11,7},{12,8},{13,9},{1... | collective-permute-start | bytes 1474568 | tf_op jit(solution)/shard_map/ppermute | solution.py:279
  23.3 1.9 %collective-permute-start.7 = (bf16[240,1024]{1,0:T(8,128)(2,1)}, bf16[240,1024]{1,0:T(8,128)(2,1)S(1)}, u32[]{:S(2)}, u32[]{:S(2)}) collective-permute-start(bf16[240,1024]{1,0:T(8,128)(2,1)} %collective-permute-done.6), channel_id=1, source_target_pairs={{4,8},{5,9},{6,10},{7,11},{8,12},{9,13},{10,14},{11,15},{12,16},{1... | collective-permute-start | bytes 1474568 | tf_op jit(solution)/shard_map/ppermute | solution.py:279
  25.2 8.3 %collective-permute-done.2.other_ref = bf16[240,1024]{1,0:T(8,128)(2,1)S(1)} collective-permute-done((bf16[240,1024]{1,0:T(8,128)(2,1)S(1)}, bf16[240,1024]{1,0:T(8,128)(2,1)S(1)}, u32[]{:S(2)}, u32[]{:S(2)}) %collective-permute-start.2) | collective-permute-done | bytes 491552 | tf_op jit(solution)/shard_map/ppermute | solution.py:279
  33.6 3.5 %collective-permute-start.3 = (bf16[240,1024]{1,0:T(8,128)(2,1)S(1)}, bf16[240,1024]{1,0:T(8,128)(2,1)S(1)}, u32[]{:S(2)}, u32[]{:S(2)}) collective-permute-start(bf16[240,1024]{1,0:T(8,128)(2,1)S(1)} %shard_map.29.up2_ref.refs_3_), channel_id=1, source_target_pairs={{0,2},{1,3},{2,0},{3,1},{4,6},{5,7},{6,4},{7,5},{8,10},{9,11},{10,... | collective-permute-start | bytes 1474568 | tf_op jit(solution)/shard_map/ppermute | solution.py:285
  38.0 1.4 %collective-permute-start.5 = (bf16[240,1024]{1,0:T(8,128)(2,1)}, bf16[240,1024]{1,0:T(8,128)(2,1)}, u32[]{:S(2)}, u32[]{:S(2)}) collective-permute-start(bf16[240,1024]{1,0:T(8,128)(2,1)} %broadcast_select_fusion.1), channel_id=1, source_target_pairs={{4,0},{5,1},{6,2},{7,3},{24,28},{25,29},{26,30},{27,31},{36,32},{3... | collective-permute-start | bytes 1474568 | tf_op jit(solution)/shard_map/ppermute | solution.py:279
  39.4 1.9 %collective-permute-start.8 = (bf16[240,1024]{1,0:T(8,128)(2,1)S(1)}, bf16[240,1024]{1,0:T(8,128)(2,1)S(1)}, u32[]{:S(2)}, u32[]{:S(2)}) collective-permute-start(bf16[240,1024]{1,0:T(8,128)(2,1)S(1)} %shard_map.29.up2_ref.refs_3_), channel_id=1, source_target_pairs={{0,1},{1,0},{2,3},{3,2},{4,5},{5,4},{6,7},{7,6},{8,9},{9,8},{10,11... | collective-permute-start | bytes 1474568 | tf_op jit(solution)/shard_map/ppermute | solution.py:285
  41.3 5.9 %collective-permute-done.3.extra_ref = bf16[240,1024]{1,0:T(8,128)(2,1)S(1)} collective-permute-done((bf16[240,1024]{1,0:T(8,128)(2,1)S(1)}, bf16[240,1024]{1,0:T(8,128)(2,1)S(1)}, u32[]{:S(2)}, u32[]{:S(2)}) %collective-permute-start.3) | collective-permute-done | bytes 491552 | tf_op jit(solution)/shard_map/ppermute | solution.py:285
  47.3 1.9 %collective-permute-start.4 = (bf16[240,1024]{1,0:T(8,128)(2,1)S(1)}, bf16[240,1024]{1,0:T(8,128)(2,1)S(1)}, u32[]{:S(2)}, u32[]{:S(2)}) collective-permute-start(bf16[240,1024]{1,0:T(8,128)(2,1)S(1)} %collective-permute-done.3.extra_ref), channel_id=1, source_target_pairs={{0,1},{1,0},{2,3},{3,2},{4,5},{5,4},{6,7},{7,6},{8,9},{9,8},{10,11... | collective-permute-start | bytes 1474568 | tf_op jit(solution)/shard_map/ppermute | solution.py:285
  49.3 1.6 %shard_map.31 = (f32[32,224]{1,0:T(8,128)S(1)}, f32[32,224]{1,0:T(8,128)S(1)}, f32[32,224]{1,0:T(8,128)S(1)}, f32[32,224]{1,0:T(8,128)S(1)}, f32[1,224]{1,0:T(1,...) custom-call(s32[1]{0:T(128)} %bitcast.3.low_ref, bf16[240,1024]{1,0:T(8,128)(2,1)S(1)} %collective-permute-done.8.extra_ref.refs_4_, ...), custom_call_target="tpu_custom_call" | custom-call | flops 436731904 | bytes 1966080 | tf_op jit(solution)/shard_map/pallas_call | solution.py:260
  50.9 1.3 %broadcast_select_fusion = (bf16[240,1024]{1,0:T(8,128)(2,1)S(1)}, bf16[240,1024]{1,0:T(8,128)(2,1)S(1)}) fusion(bf16[240,1024]{1,0:T(8,128)(2,1)} %collective-permute-done.5, bf16[240,1024]{1,0:T(8,128)(2,1)} %collective-permute-done.6, pred[]{:T(512)S(6)} %eq.28, bf16[240,1024]{1,0:T(8,128)(2,1)S(1)} %copy-done.2, pred[]{:T(512)S(6)} %eq.25), kind=kLoop, calls=%fused_computation | loop fusion | flops 491520 | bytes 2457602 | tf_op jit(solution)/shard_map/jit(_where)/select_n | solution.py:302
  52.2 2.0 %shard_map.32 = (f32[32,224]{1,0:T(8,128)S(1)}, f32[32,224]{1,0:T(8,128)S(1)}, f32[32,224]{1,0:T(8,128)S(1)}, f32[32,224]{1,0:T(8,128)S(1)}, f32[32,224]{1,0:T(8...) custom-call(bf16[240,1024]{1,0:T(8,128)(2,1)S(1)} %shard_map.28.zero_ref.refs_0_, ...), custom_call_target="tpu_custom_call" | custom-call | flops 545914880 | bytes 2457600 | tf_op jit(solution)/shard_map/pallas_call | solution.py:174
  54.2 1.7 %shard_map.33 = (f32[32,224]{1,0:T(8,128)S(1)}, f32[32,224]{1,0:T(8,128)S(1)}, f32[32,224]{1,0:T(8,128)S(1)}, f32[32,224]{1,0:T(8,128)S(1)}, f32[32,224]{1,0:T(8,128)S(1)}, /*index=5*/f32[32,224]{1,0:T(8,128)S(1)}) custom-call(s32[1]{0:T(128)} %bitcast.low_ref, bf16[240,1024]{1,0:T(8,128)(2,1)S(1)} %collective-permute-done.3.extra_ref, ...), custom_call_target="tpu_custom_call" | custom-call | flops 436731904 | bytes 2949120 | tf_op jit(solution)/shard_map/pallas_call | solution.py:215
  56.0 1.7 %shard_map.34 = (f32[32,224]{1,0:T(8,128)S(1)}, f32[32,224]{1,0:T(8,128)S(1)}, f32[32,224]{1,0:T(8,128)S(1)}, f32[32,224]{1,0:T(8,128)S(1)}, f32[32,224]{1,0:T(8,128)S(1)}, /*index=5*/f32[32,224]{1,0:T(8,128)S(1)}) custom-call(s32[1]{0:T(128)} %bitcast.low_ref, bf16[240,1024]{1,0:T(8,128)(2,1)S(1)} %collective-permute-done.4.extra_ref, ...), custom_call_target="tpu_custom_call" | custom-call | flops 436731904 | bytes 2949120 | tf_op jit(solution)/shard_map/pallas_call | solution.py:215
  57.8 2.4 %collective-permute-start.12 = (f32[64,224]{1,0:T(8,128)S(1)}, f32[64,224]{1,0:T(8,128)S(1)}, u32[]{:S(2)}, u32[]{:S(2)}) collective-permute-start(f32[64,224]{1,0:T(8,128)S(1)} %pad_maximum_fusion.2), channel_id=1, source_target_pairs={{0,1},{1,0},{2,3},{3,2},{4,5},{5,4},{6,7},{7,6},{8,9},{9,8},{10,11... | collective-permute-start | bytes 172040 | tf_op jit(solution)/shard_map/ppermute | solution.py:285
  60.2 4.6 %collective-permute-start.9 = (f32[64,224]{1,0:T(8,128)S(1)}, f32[64,224]{1,0:T(8,128)S(1)}, u32[]{:S(2)}, u32[]{:S(2)}) collective-permute-start(f32[64,224]{1,0:T(8,128)S(1)} %pad_maximum_fusion), channel_id=1, source_target_pairs={{0,4},{1,5},{2,6},{3,7},{4,8},{5,9},{6,10},{7,11},{8,12},{9,13},{1... | collective-permute-start | bytes 172040 | tf_op jit(solution)/shard_map/ppermute | solution.py:282
  64.8 9.9 %collective-permute-start.10 = (f32[64,224]{1,0:T(8,128)S(1)}, f32[64,224]{1,0:T(8,128)S(1)}, u32[]{:S(2)}, u32[]{:S(2)}) collective-permute-start(f32[64,224]{1,0:T(8,128)S(1)} %pad_maximum_fusion.1), channel_id=1, source_target_pairs={{4,0},{5,1},{6,2},{7,3},{8,4},{9,5},{10,6},{11,7},{12,8},{13,9},{1... | collective-permute-start | bytes 172040 | tf_op jit(solution)/shard_map/ppermute | solution.py:282
  74.6 3.3 %collective-permute-start.13 = (f32[32,224]{1,0:T(8,128)S(1)}, f32[32,224]{1,0:T(8,128)S(1)}, u32[]{:S(2)}, u32[]{:S(2)}) collective-permute-start(f32[32,224]{1,0:T(8,128)S(1)} %slice_add_fusion.2), channel_id=1, source_target_pairs={{0,2},{1,3},{2,0},{3,1},{4,6},{5,7},{6,4},{7,5},{8,10},{9,11},{10,... | collective-permute-start | bytes 86024 | tf_op jit(solution)/shard_map/ppermute | solution.py:285
  78.0 2.7 %collective-permute-start.11 = (f32[32,224]{1,0:T(8,128)S(1)}, f32[32,224]{1,0:T(8,128)S(1)}, u32[]{:S(2)}, u32[]{:S(2)}) collective-permute-start(f32[32,224]{1,0:T(8,128)S(1)} %get-tuple-element.58), channel_id=1, source_target_pairs={{8,0},{9,1},{10,2},{11,3},{12,4},{13,5},{14,6},{15,7},{16,8},{17,9... | collective-permute-start | bytes 86024 | tf_op jit(solution)/shard_map/ppermute | solution.py:282
  81.5 5.2 %collective-permute-start.14 = (f32[32,224]{1,0:T(8,128)S(1)}, f32[32,224]{1,0:T(8,128)S(1)}, u32[]{:S(2)}, u32[]{:S(2)}) collective-permute-start(f32[32,224]{1,0:T(8,128)S(1)} %get-tuple-element.64), channel_id=1, source_target_pairs={{0,8},{1,9},{2,10},{3,11},{4,12},{5,13},{6,14},{7,15},{8,16},{9,17... | collective-permute-start | bytes 86024 | tf_op jit(solution)/shard_map/ppermute | solution.py:282
  86.7 11.9 %collective-permute-done.14 = f32[32,224]{1,0:T(8,128)S(1)} collective-permute-done((f32[32,224]{1,0:T(8,128)S(1)}, f32[32,224]{1,0:T(8,128)S(1)}, u32[]{:S(2)}, u32[]{:S(2)}) %collective-permute-start.14) | collective-permute-done | bytes 28704 | tf_op jit(solution)/shard_map/ppermute | solution.py:282
  (32 shorter events, 4.0 us)
Async XLA Ops:
  0.8 1.0 %copy-start = (bf16[224,1024]{1,0:T(8,128)(2,1)S(1)}, bf16[224,1024]{1,0:T(8,128)(2,1)}, u32[]{:S(2)}) copy-start(bf16[224,1024]{1,0:T(8,128)(2,1)} %spectra_ref.1) | copy-start | bytes 1376260
  1.9 15.5 %collective-permute-start.1 = (bf16[240,1024]{1,0:T(8,128)(2,1)S(1)}, bf16[240,1024]{1,0:T(8,128)(2,1)S(1)}, u32[]{:S(2)}, u32[]{:S(2)}) collective-permute-start(bf16[240,1024]{1,0:T(8,128)(2,1)S(1)} %shard_map.28.zero_ref.refs_0_), channel_id=1, source_target_pairs={{4,0},{5,1},{6,2},{7,3},{8,4},{9,5},{10,6},{11,7},{12,8},{13,9},{1... | collective-permute-start | bytes 1474568 | tf_op jit(solution)/shard_map/ppermute | solution.py:279
  3.9 19.4 %collective-permute-start.6 = (bf16[240,1024]{1,0:T(8,128)(2,1)S(1)}, bf16[240,1024]{1,0:T(8,128)(2,1)}, u32[]{:S(2)}, u32[]{:S(2)}) collective-permute-start(bf16[240,1024]{1,0:T(8,128)(2,1)S(1)} %shard_map.28.zero_ref.refs_0_), channel_id=1, source_target_pairs={{0,4},{1,5},{2,6},{3,7},{4,8},{5,9},{6,10},{7,11},{8,12},{9,13},{1... | collective-permute-start | bytes 1474568 | tf_op jit(solution)/shard_map/ppermute | solution.py:279
  8.1 17.1 %collective-permute-start = (bf16[240,1024]{1,0:T(8,128)(2,1)S(1)}, bf16[240,1024]{1,0:T(8,128)(2,1)S(1)}, u32[]{:S(2)}, u32[]{:S(2)}) collective-permute-start(bf16[240,1024]{1,0:T(8,128)(2,1)S(1)} %shard_map.28.zero_ref.refs_0_), channel_id=1, source_target_pairs={{504,0},{505,1},{506,2},{507,3},{508,4},{509,5},{510,6},{511,7},{3... | collective-permute-start | bytes 1474568 | tf_op jit(solution)/shard_map/ppermute | solution.py:279
  17.4 16.1 %copy-start.1 = (bf16[240,1024]{1,0:T(8,128)(2,1)}, bf16[240,1024]{1,0:T(8,128)(2,1)S(1)}, u32[]{:S(2)}) copy-start(bf16[240,1024]{1,0:T(8,128)(2,1)S(1)} %collective-permute-done.1) | copy-start | bytes 1474564
  17.4 16.1 %collective-permute-start.2 = (bf16[240,1024]{1,0:T(8,128)(2,1)S(1)}, bf16[240,1024]{1,0:T(8,128)(2,1)S(1)}, u32[]{:S(2)}, u32[]{:S(2)}) collective-permute-start(bf16[240,1024]{1,0:T(8,128)(2,1)S(1)} %collective-permute-done.1), channel_id=1, source_target_pairs={{4,0},{5,1},{6,2},{7,3},{8,4},{9,5},{10,6},{11,7},{12,8},{13,9},{1... | collective-permute-start | bytes 1474568 | tf_op jit(solution)/shard_map/ppermute | solution.py:279
  23.3 25.9 %collective-permute-start.7 = (bf16[240,1024]{1,0:T(8,128)(2,1)}, bf16[240,1024]{1,0:T(8,128)(2,1)S(1)}, u32[]{:S(2)}, u32[]{:S(2)}) collective-permute-start(bf16[240,1024]{1,0:T(8,128)(2,1)} %collective-permute-done.6), channel_id=1, source_target_pairs={{4,8},{5,9},{6,10},{7,11},{8,12},{9,13},{10,14},{11,15},{12,16},{1... | collective-permute-start | bytes 1474568 | tf_op jit(solution)/shard_map/ppermute | solution.py:279
  33.6 13.7 %collective-permute-start.3 = (bf16[240,1024]{1,0:T(8,128)(2,1)S(1)}, bf16[240,1024]{1,0:T(8,128)(2,1)S(1)}, u32[]{:S(2)}, u32[]{:S(2)}) collective-permute-start(bf16[240,1024]{1,0:T(8,128)(2,1)S(1)} %shard_map.29.up2_ref.refs_3_), channel_id=1, source_target_pairs={{0,2},{1,3},{2,0},{3,1},{4,6},{5,7},{6,4},{7,5},{8,10},{9,11},{10,... | collective-permute-start | bytes 1474568 | tf_op jit(solution)/shard_map/ppermute | solution.py:285
  38.0 11.3 %collective-permute-start.5 = (bf16[240,1024]{1,0:T(8,128)(2,1)}, bf16[240,1024]{1,0:T(8,128)(2,1)}, u32[]{:S(2)}, u32[]{:S(2)}) collective-permute-start(bf16[240,1024]{1,0:T(8,128)(2,1)} %broadcast_select_fusion.1), channel_id=1, source_target_pairs={{4,0},{5,1},{6,2},{7,3},{24,28},{25,29},{26,30},{27,31},{36,32},{3... | collective-permute-start | bytes 1474568 | tf_op jit(solution)/shard_map/ppermute | solution.py:279
  39.4 9.9 %collective-permute-start.8 = (bf16[240,1024]{1,0:T(8,128)(2,1)S(1)}, bf16[240,1024]{1,0:T(8,128)(2,1)S(1)}, u32[]{:S(2)}, u32[]{:S(2)}) collective-permute-start(bf16[240,1024]{1,0:T(8,128)(2,1)S(1)} %shard_map.29.up2_ref.refs_3_), channel_id=1, source_target_pairs={{0,1},{1,0},{2,3},{3,2},{4,5},{5,4},{6,7},{7,6},{8,9},{9,8},{10,11... | collective-permute-start | bytes 1474568 | tf_op jit(solution)/shard_map/ppermute | solution.py:285
  47.3 8.7 %collective-permute-start.4 = (bf16[240,1024]{1,0:T(8,128)(2,1)S(1)}, bf16[240,1024]{1,0:T(8,128)(2,1)S(1)}, u32[]{:S(2)}, u32[]{:S(2)}) collective-permute-start(bf16[240,1024]{1,0:T(8,128)(2,1)S(1)} %collective-permute-done.3.extra_ref), channel_id=1, source_target_pairs={{0,1},{1,0},{2,3},{3,2},{4,5},{5,4},{6,7},{7,6},{8,9},{9,8},{10,11... | collective-permute-start | bytes 1474568 | tf_op jit(solution)/shard_map/ppermute | solution.py:285
  49.3 1.6 %copy-start.2 = (bf16[240,1024]{1,0:T(8,128)(2,1)S(1)}, bf16[240,1024]{1,0:T(8,128)(2,1)}, u32[]{:S(2)}) copy-start(bf16[240,1024]{1,0:T(8,128)(2,1)} %copy-done.1) | copy-start | bytes 1474564
  57.8 16.9 %collective-permute-start.12 = (f32[64,224]{1,0:T(8,128)S(1)}, f32[64,224]{1,0:T(8,128)S(1)}, u32[]{:S(2)}, u32[]{:S(2)}) collective-permute-start(f32[64,224]{1,0:T(8,128)S(1)} %pad_maximum_fusion.2), channel_id=1, source_target_pairs={{0,1},{1,0},{2,3},{3,2},{4,5},{5,4},{6,7},{7,6},{8,9},{9,8},{10,11... | collective-permute-start | bytes 172040 | tf_op jit(solution)/shard_map/ppermute | solution.py:285
  60.2 20.6 %collective-permute-start.9 = (f32[64,224]{1,0:T(8,128)S(1)}, f32[64,224]{1,0:T(8,128)S(1)}, u32[]{:S(2)}, u32[]{:S(2)}) collective-permute-start(f32[64,224]{1,0:T(8,128)S(1)} %pad_maximum_fusion), channel_id=1, source_target_pairs={{0,4},{1,5},{2,6},{3,7},{4,8},{5,9},{6,10},{7,11},{8,12},{9,13},{1... | collective-permute-start | bytes 172040 | tf_op jit(solution)/shard_map/ppermute | solution.py:282
  64.8 16.0 %collective-permute-start.10 = (f32[64,224]{1,0:T(8,128)S(1)}, f32[64,224]{1,0:T(8,128)S(1)}, u32[]{:S(2)}, u32[]{:S(2)}) collective-permute-start(f32[64,224]{1,0:T(8,128)S(1)} %pad_maximum_fusion.1), channel_id=1, source_target_pairs={{4,0},{5,1},{6,2},{7,3},{8,4},{9,5},{10,6},{11,7},{12,8},{13,9},{1... | collective-permute-start | bytes 172040 | tf_op jit(solution)/shard_map/ppermute | solution.py:282
  74.6 6.1 %collective-permute-start.13 = (f32[32,224]{1,0:T(8,128)S(1)}, f32[32,224]{1,0:T(8,128)S(1)}, u32[]{:S(2)}, u32[]{:S(2)}) collective-permute-start(f32[32,224]{1,0:T(8,128)S(1)} %slice_add_fusion.2), channel_id=1, source_target_pairs={{0,2},{1,3},{2,0},{3,1},{4,6},{5,7},{6,4},{7,5},{8,10},{9,11},{10,... | collective-permute-start | bytes 86024 | tf_op jit(solution)/shard_map/ppermute | solution.py:285
  78.0 8.7 %collective-permute-start.11 = (f32[32,224]{1,0:T(8,128)S(1)}, f32[32,224]{1,0:T(8,128)S(1)}, u32[]{:S(2)}, u32[]{:S(2)}) collective-permute-start(f32[32,224]{1,0:T(8,128)S(1)} %get-tuple-element.58), channel_id=1, source_target_pairs={{8,0},{9,1},{10,2},{11,3},{12,4},{13,5},{14,6},{15,7},{16,8},{17,9... | collective-permute-start | bytes 86024 | tf_op jit(solution)/shard_map/ppermute | solution.py:282
  80.8 5.9 %collective-permute-start.15 = (f32[32,224]{1,0:T(8,128)S(1)}, f32[32,224]{1,0:T(8,128)S(1)}, u32[]{:S(2)}, u32[]{:S(2)}) collective-permute-start(f32[32,224]{1,0:T(8,128)S(1)} %get-tuple-element.63), channel_id=1, source_target_pairs={{0,504},{1,505},{2,506},{3,507},{4,508},{5,509},{6,510},{7,511},{2... | collective-permute-start | bytes 86024 | tf_op jit(solution)/shard_map/ppermute | solution.py:282
  81.5 17.2 %collective-permute-start.14 = (f32[32,224]{1,0:T(8,128)S(1)}, f32[32,224]{1,0:T(8,128)S(1)}, u32[]{:S(2)}, u32[]{:S(2)}) collective-permute-start(f32[32,224]{1,0:T(8,128)S(1)} %get-tuple-element.64), channel_id=1, source_target_pairs={{0,8},{1,9},{2,10},{3,11},{4,12},{5,13},{6,14},{7,15},{8,16},{9,17... | collective-permute-start | bytes 86024 | tf_op jit(solution)/shard_map/ppermute | solution.py:282
